TPU v7x, 512 devices: a whole 4x4x16 slice. The times are simulated.
512 devices in a mesh: ctx: 32 (over z_lo, y), grp: 16 (over x, z_hi, core).
Axes of the slice: x: 4, y: 4, z: 16 (z_hi: 2, z_lo: 8; z = z_hi * 8 + z_lo), core: 2. Of those that a mesh axis runs over, the one named last changes fastest.
Arguments:
- q_nope: bfloat16 [256, 128, 128], P(None, 'ctx'), may hold values from -6 to 6
- q_rope: bfloat16 [256, 128, 64], P(None, 'ctx'), may hold values from -720 to 720
- w_uk: bfloat16 [128, 128, 512], P('ctx'), may hold values from -0.5 to 0.5
- w_uv: bfloat16 [128, 512, 128], P('ctx'), may hold values from -0.375 to 0.375
- prompt: bfloat16 [6144, 576], P('grp'), may hold values from -12 to 12
- w_out: bfloat16 [16384, 7168], P('ctx', 'grp'), may hold values from -0.0625 to 0.0625
- residual: bfloat16 [256, 7168], P('ctx', 'grp'), may hold values from -3 to 3
- routes: int32 [256, 8], P('ctx'), may hold values from 0 to 31, all different within a row; in each aligned block of 8 rows (0 to 7, 8 to 15, ...) at most 4 rows name the same one
- route_scores: float32 [256, 8], P('ctx'), may hold values from 0.05 to 1
- expert_gate: bfloat16 [32, 7168, 1024], P('ctx', 'grp'), may hold values from -0.0625 to 0.0625
- expert_up: bfloat16 [32, 7168, 1024], P('ctx', 'grp'), may hold values from -0.0625 to 0.0625
- expert_down: bfloat16 [32, 1024, 7168], P('ctx', None, 'grp'), may hold values from -0.1875 to 0.1875
Outputs:
- layer_out: bfloat16 [256, 7168], P('ctx', 'grp')
Inputs may be any that keep to these rules, and one draw needn't show every extreme that they name: `routes`: in each aligned block of 8 rows no expert is named by more than 4 rows, a bound that some block reaches; the 8 experts of a row differ.
All inputs are finite; a program needn't handle non-finite values.
Results may differ from a plain program's by a relative error of at most 0.0163.
Values may be sent and summed in bfloat16 or wider, within the bound.
A program may use at most 64 MiB of HBM per device.

v0:
```python
import jax
import jax.numpy as jnp
from jax import lax
from jax.sharding import PartitionSpec as P

NOPE = 128
ROPE = 64
LAT = 512
VDIM = 128
CAP = 4
route_factor = 2.5


def per_device(
    q_nope,
    q_rope,
    w_uk,
    w_uv,
    prompt,
    w_out,
    residual,
    routes,
    route_scores,
    expert_gate,
    expert_up,
    expert_down,
):
    score_scale = (NOPE + ROPE) ** (-0.5)
    q_latent = jnp.einsum("rhn,hnl->rhl", q_nope, w_uk, preferred_element_type=jnp.float32).astype(
        jnp.bfloat16
    )
    queries = jnp.concatenate([q_latent, q_rope], axis=-1)
    head_uv = w_uv.astype(jnp.float32)
    head_cols = queries.shape[1] * VDIM
    all_keys = lax.all_gather(prompt, "grp", axis=0, tiled=True)
    row_share = queries.shape[0] // lax.axis_size("grp")
    own_queries = lax.dynamic_slice_in_dim(queries, lax.axis_index("grp") * row_share, row_share, 0)
    scores = (
        jnp.einsum("rhc,jc->rhj", own_queries, all_keys, preferred_element_type=jnp.float32)
        * score_scale
    )
    top_score = jnp.max(scores, axis=-1)
    raised = jnp.exp(scores - top_score[..., None])
    denominator = jnp.sum(raised, axis=-1)
    weighted = jnp.einsum(
        "rhj,jl->rhl",
        raised.astype(jnp.bfloat16),
        all_keys[:, :LAT],
        preferred_element_type=jnp.float32,
    )
    values = jnp.einsum("rhl,hlv->rhv", weighted, head_uv, precision=lax.Precision.HIGHEST)
    top_score, denominator, values = (top_score, denominator, values)
    own_rows = (values / denominator[..., None]).astype(jnp.bfloat16).reshape(row_share, head_cols)
    attended = lax.all_gather(own_rows, "grp", axis=0, tiled=True)
    local_rows = residual.shape[0]
    projected = lax.psum_scatter(
        jnp.dot(attended, w_out, preferred_element_type=jnp.float32),
        "ctx",
        scatter_dimension=0,
        tiled=True,
    )
    hidden = residual.astype(jnp.float32) + projected
    moe_input = hidden.astype(jnp.bfloat16)
    gate_weights = route_factor * route_scores / jnp.sum(route_scores, axis=-1, keepdims=True)
    top_count = routes.shape[1]
    experts = expert_gate.shape[0] * lax.axis_size("ctx")
    flat_routes = routes.reshape(-1)
    onehot = (flat_routes[:, None] == jnp.arange(experts, dtype=jnp.int32)[None, :]).astype(
        jnp.int32
    )
    before = jnp.cumsum(onehot, axis=0) - onehot
    slot_index = jnp.sum(before * onehot, axis=1)
    target = flat_routes * CAP + slot_index
    select = (target[:, None] == jnp.arange(experts * CAP, dtype=jnp.int32)[None, :]).astype(
        jnp.float32
    )
    row_of = jnp.arange(local_rows * top_count, dtype=jnp.int32) // top_count
    row_pick = (row_of[:, None] == jnp.arange(local_rows, dtype=jnp.int32)[None, :]).astype(
        jnp.float32
    )
    slot_rows = jnp.dot(select.T, row_pick, precision=lax.Precision.HIGHEST)
    outgoing = jnp.dot(
        slot_rows.astype(jnp.bfloat16), moe_input, preferred_element_type=jnp.float32
    ).astype(jnp.bfloat16)
    outgoing = outgoing.reshape(experts, 1, CAP, moe_input.shape[1])
    slot_weights = jnp.dot(
        row_pick.T, select * gate_weights.reshape(-1)[:, None], precision=lax.Precision.HIGHEST
    )
    arrived = lax.all_to_all(outgoing, "ctx", split_axis=0, concat_axis=1, tiled=True)
    gate_part = jnp.einsum(
        "escd,edf->escf", arrived, expert_gate, preferred_element_type=jnp.float32
    )
    up_part = jnp.einsum("escd,edf->escf", arrived, expert_up, preferred_element_type=jnp.float32)
    gate_sum, up_sum = lax.psum((gate_part, up_part), "grp")
    activated = (jax.nn.silu(gate_sum) * up_sum).astype(jnp.bfloat16)
    result = jnp.einsum(
        "escf,efd->escd", activated, expert_down, preferred_element_type=jnp.float32
    ).astype(jnp.bfloat16)
    returned = lax.all_to_all(result, "ctx", split_axis=1, concat_axis=0, tiled=True)
    returned = returned.reshape(experts * CAP, moe_input.shape[1]).astype(jnp.float32)
    combined = jnp.dot(slot_weights, returned, precision=lax.Precision.HIGHEST)
    return (hidden + combined).astype(jnp.bfloat16)


def solution(mesh):
    in_specs = (
        P(None, "ctx", None),
        P(None, "ctx", None),
        P("ctx", None, None),
        P("ctx", None, None),
        P("grp", None),
        P("ctx", "grp"),
        P("ctx", "grp"),
        P("ctx", None),
        P("ctx", None),
        P("ctx", "grp", None),
        P("ctx", "grp", None),
        P("ctx", None, "grp"),
    )
    out_specs = P("ctx", "grp")
    return jax.shard_map(
        per_device, mesh=mesh, in_specs=in_specs, out_specs=out_specs, check_vma=False
    )
```

profile of v0, /device:TPU:8, one launch (start us, length us, event | category | flops | bytes accessed | tf_op | source)
XLA Modules:
  0.0 793.5 jit_solution(4318295882476667328)
XLA Ops:
  6.5 0.0 copy-start
  6.5 0.0 copy-start.5
  6.5 0.0 all-gather.2.cloned.1.call-start
  6.5 0.7 all-gather.2.cloned.1.call-update
  7.3 0.0 reduce-scatter.2.cloned.1.call-start
  7.3 1.6 fusion.8
  8.9 171.5 %all-gather.2.cloned.1.call-done = bf16[6144,576]{0,1:T(8,128)(2,1)} async-done(((bf16[384,576]{0,1:T(8,128)(2,1)}), bf16[6144,576]{0,1:T(8,128)(2,1)}) %all-gather.2.cloned.1.call-update) | async-done | bytes 7077904 | tf_op jit(solution)/shard_map/all_gather | solution.py:35
  180.4 0.0 copy-done.5
  180.4 0.0 copy-start.1
  180.4 4.4 fusion.42
  184.8 0.4 fusion.6
  185.2 0.3 copy-done.1
  185.5 0.0 copy-start.3
  185.5 0.0 copy-start.4
  185.5 2.0 fusion.5
  187.6 0.0 copy-done.3
  187.6 0.0 copy-start.9
  187.6 0.0 copy-start.7
  187.6 0.3 fusion.12
  187.9 35.3 %all_gather.7 = bf16[256,512]{1,0:T(8,128)(2,1)S(1)} all-gather(bf16[16,512]{1,0:T(8,128)(2,1)S(1)} %bitcast.63), channel_id=1, replica_groups=mesh['ctx'=32,'grp'=16] {'grp'}, dimensions={0}, use_global_device_ids=true | all-gather | bytes 278528 | tf_op jit(solution)/shard_map/all_gather | solution.py:54
  223.3 0.0 copy-done.4
  223.3 1.1 fusion.43
  224.4 0.0 copy-start.2
  224.4 0.0 reduce-scatter.2.cloned.1.call-update
  224.4 0.0 all-reduce.3.cloned.1.call-start
  224.4 0.0 copy-done.9
  224.5 0.1 reshape.68
  224.5 0.1 fusion.29
  224.6 0.1 reduce_window_sum.11
  224.7 0.2 select_reduce_fusion
  224.9 0.3 convolution_convert_fusion.3
  225.2 228.0 %reduce-scatter.2.cloned.1.call-done = f32[8,448]{1,0:T(8,128)} async-done(((f32[256,448]{1,0:T(8,128)}), f32[8,448]{1,0:T(8,128)}) %reduce-scatter.2.cloned.1.call-update) | async-done | bytes 14352 | tf_op jit(solution)/shard_map/reduce_scatter | solution.py:56
  453.2 0.0 copy-done.7
  453.2 1.0 convolution_convert_fusion.2
  454.1 0.1 copy.25
  454.3 24.6 %all_to_all.8 = bf16[32,1,4,448]{3,2,1,0:T(4,128)(2,1)S(1)} all-to-all(bf16[32,1,4,448]{3,2,1,0:T(4,128)(2,1)S(1)} %bitcast.62), channel_id=1, replica_groups=mesh['ctx'=32,'grp'=16] {'ctx'}, dimensions={0} | all-to-all | bytes 229376 | tf_op jit(solution)/shard_map/all_to_all | solution.py:89
  478.9 0.0 copy-done
  478.9 1.1 convolution_bitcast_fusion
  480.0 0.0 copy-done.2
  480.0 0.0 copy-start.8
  480.0 0.0 copy-start.10
  480.0 1.1 convolution_bitcast_fusion.1
  481.1 0.0 all-reduce.3.cloned.1.call-update
  481.1 0.0 copy-done.8
  481.1 0.1 reduce_sum.29
  481.2 283.5 %all-reduce.3.cloned.1.call-done = (f32[1,32,4,1024]{3,1,2,0:T(8,128)}, f32[1,32,4,1024]{3,1,2,0:T(8,128)}) async-done(((f32[1,32,4,1024]{3,1,2,0:T(8,128)}, f32[1,32,4,1024]{3,1,2,0:T(8,128)}), (f32[1,32,4,1024]{3,1,2,0:T(8,128)}, f32[1,32,4,1024]{3,1,2,0:T(8,128)})) %all-reduce.3.cloned.1.call-update) | async-done | bytes 1048592 | tf_op jit(solution)/shard_map/psum | solution.py:94
  764.7 0.0 copy-done.10
  764.7 0.0 copy-start.6
  764.7 1.7 fusion.9
  766.4 0.7 copy.28
  767.1 7.0 all-to-all-start.1
  774.2 0.1 multiply_divide_fusion
  774.2 0.1 mul.53
  774.3 0.3 fusion.27
  774.6 11.6 %all-to-all-done.1 = bf16[1,32,4,448]{3,2,0,1:T(4,128)(2,1)S(1)} async-done(((bf16[1,32,4,448]{3,2,0,1:T(4,128)(2,1)}), bf16[1,32,4,448]{3,2,0,1:T(4,128)(2,1)S(1)}, u32[]{:S(2)}, u32[]{:S(2)}) %all-to-all-start.1) | async-done | bytes 114720 | tf_op jit(solution)/shard_map/all_to_all | solution.py:99
  786.2 0.1 reshape.75
  786.2 0.0 copy-done.6
  786.2 0.8 fusion.13
  (3 shorter events, 0.1 us)
Async XLA Ops:
  6.5 472.3 %copy-start = (bf16[1,448,1024]{2,1,0:T(8,128)(2,1)S(1)}, bf16[1,448,1024]{2,1,0:T(8,128)(2,1)}, u32[]{:S(2)}) copy-start(bf16[1,448,1024]{2,1,0:T(8,128)(2,1)} %param.22) | copy-start | bytes 2752516
  6.5 173.9 %copy-start.5 = (bf16[256,4,64]{0,2,1:T(8,128)(2,1)S(1)}, bf16[256,4,64]{0,2,1:T(8,128)(2,1)}, u32[]{:S(2)}) copy-start(bf16[256,4,64]{0,2,1:T(8,128)(2,1)} %param.13) | copy-start | bytes 393220
  6.5 173.9 %all-gather.2.cloned.1.call-start = ((), (), s32[]{:S(2)}) async-start(), calls=%async_computation.3 | async-start | bytes 7520256 | tf_op jit(solution)/shard_map/all_gather | solution.py:35
  7.3 445.9 %reduce-scatter.2.cloned.1.call-start = ((), (), s32[]{:S(2)}) async-start(), calls=%async_computation.4 | async-start | bytes 540672 | tf_op jit(solution)/shard_map/reduce_scatter | solution.py:56
  180.4 5.1 copy-start.1
  185.5 2.0 copy-start.3
  185.5 37.7 %copy-start.4 = (bf16[512,448]{0,1:T(8,128)(2,1)S(1)}, bf16[512,448]{0,1:T(8,128)(2,1)}, u32[]{:S(2)}) copy-start(bf16[512,448]{0,1:T(8,128)(2,1)} %param.17) | copy-start | bytes 1376260
  187.6 36.9 %copy-start.9 = (s32[8,8]{1,0:T(8,128)S(1)}, s32[8,8]{1,0:T(8,128)}, u32[]{:S(2)}) copy-start(s32[8,8]{1,0:T(8,128)} %param.19) | copy-start | bytes 772
  187.6 265.6 %copy-start.7 = (bf16[8,448]{1,0:T(8,128)(2,1)S(1)}, bf16[8,448]{1,0:T(8,128)(2,1)}, u32[]{:S(2)}) copy-start(bf16[8,448]{1,0:T(8,128)(2,1)} %param.18) | copy-start | bytes 21508
  224.4 255.6 %copy-start.2 = (bf16[1,448,1024]{2,1,0:T(8,128)(2,1)S(1)}, bf16[1,448,1024]{2,1,0:T(8,128)(2,1)}, u32[]{:S(2)}) copy-start(bf16[1,448,1024]{2,1,0:T(8,128)(2,1)} %param.21) | copy-start | bytes 2752516
  224.4 540.3 %all-reduce.3.cloned.1.call-start = ((), (), s32[]{:S(2)}) async-start(), calls=%async_computation.5 | async-start | bytes 2097152 | tf_op jit(solution)/shard_map/psum | solution.py:94
  480.0 1.1 copy-start.8
  480.0 284.7 %copy-start.10 = (bf16[1,1024,448]{1,2,0:T(8,128)(2,1)S(1)}, bf16[1,1024,448]{1,2,0:T(8,128)(2,1)}, u32[]{:S(2)}) copy-start(bf16[1,1024,448]{1,2,0:T(8,128)(2,1)} %param.23) | copy-start | bytes 2752516
  764.7 21.5 %copy-start.6 = (f32[8,448]{1,0:T(8,128)S(1)}, f32[8,448]{1,0:T(8,128)}, u32[]{:S(2)}) copy-start(f32[8,448]{1,0:T(8,128)} %reduce-scatter.2.cloned.1.call-done) | copy-start | bytes 43012
  767.1 19.1 %all-to-all-start.1 = ((bf16[1,32,4,448]{3,2,0,1:T(4,128)(2,1)}), bf16[1,32,4,448]{3,2,0,1:T(4,128)(2,1)S(1)}, u32[]{:S(2)}, u32[]{:S(2)}) async-start(bf16[1,32,4,448]{3,2,0,1:T(4,128)(2,1)} %copy.28), calls=%async_computation.2 | async-start | bytes 262144 | tf_op jit(solution)/shard_map/all_to_all | solution.py:99
Sparse Core Ops, SparseCore 0:
  10.5 169.9 all-gather.1
  224.5 228.5 reduce-scatter.1
  481.2 283.4 all-reduce.2
where the time goes:
time: 794 us
  waiting for transfers between devices  695 us (88%)
  blocking collectives  59.9 us (8%)
  matrix products  15.5 us (2%)
  between operations  13.2 us (2%)
    psum x1, waiting for transfers between devices, per_device(): gate_sum, up_sum = lax.psum((gate_part, up_part), 'grp')  283 us
    reduce_scatter x1, waiting for transfers between devices, per_device(): lax.psum_scatter(jnp.dot(attended, w_out, preferred_element_type=jnp.floa...  228 us
    all_gather x1, waiting for transfers between devices, per_device(): all_keys = lax.all_gather(prompt, 'grp', axis=0, tiled=True)  172 us
    all_gather x1, blocking collectives, per_device(): attended = lax.all_gather(own_rows, 'grp', axis=0, tiled=True)  35.3 us
    all_to_all x1, blocking collectives, per_device(): lax.all_to_all(outgoing, 'ctx', split_axis=0, concat_axis=1, tiled=True)  24.6 us
  transfers between devices with their start and end apart: 4, of which 4 were waited for; matrix products, arithmetic and copies ran while one was open for 0% of the time, Pallas kernels for 0%

commit v1 on v0

--- a/solution.py
+++ b/solution.py
@@ -32,7 +32,9 @@
     queries = jnp.concatenate([q_latent, q_rope], axis=-1)
     head_uv = w_uv.astype(jnp.float32)
     head_cols = queries.shape[1] * VDIM
-    all_keys = lax.all_gather(prompt, "grp", axis=0, tiled=True)
+    all_keys = jnp.concatenate(
+        lax.all_to_all(jnp.stack([prompt] * lax.axis_size("grp")), "grp", 0, 0), axis=0
+    )
     row_share = queries.shape[0] // lax.axis_size("grp")
     own_queries = lax.dynamic_slice_in_dim(queries, lax.axis_index("grp") * row_share, row_share, 0)
     scores = (

time: 794 us -> 1010 us (1.27)
  blocking collectives: 59.9 us -> 179 us
  waiting for transfers between devices: 695 us -> 743 us
  local copies, waits for them, and re-layouts: 1.51 us -> 35.3 us
  starting transfers between devices: 7.12 us -> 25 us
    all_to_all x0 -> x1, waiting for transfers between devices: none -> 179 us  [per_device(): lax.all_to_all(jnp.stack([prompt] * lax.axis_size('grp')), 'grp', 0, 0)]
    all_gather x1 -> x0, waiting for transfers between devices: 172 us -> none  [per_device(): all_keys = lax.all_gather(prompt, 'grp', axis=0, tiled=True)]
    all_gather x1, blocking collectives: 35.3 us -> 155 us  [per_device(): attended = lax.all_gather(own_rows, 'grp', axis=0, tiled=True)]
    reduce_scatter x1, waiting for transfers between devices: 228 us -> 268 us  [per_device(): lax.psum_scatter(jnp.dot(attended, w_out, preferred_element_type=jnp.floa...]
    reshape x0 -> x2, local copies, waits for them, and re-layouts: none -> 18.2 us  [per_device(): jnp.concatenate(lax.all_to_all(jnp.stack([prompt] * lax.axis_size('grp'))...]
    all_to_all x0 -> x1, starting transfers between devices: none -> 17.8 us  [per_device(): lax.all_to_all(jnp.stack([prompt] * lax.axis_size('grp')), 'grp', 0, 0)]
where the time goes in v1:
time: 1010 us
  waiting for transfers between devices  743 us (74%)
  blocking collectives  179 us (18%)
  local copies, waits for them, and re-layouts  35.3 us (3%)
  starting transfers between devices  25 us (2%)
  between operations  13.6 us (1%)
  matrix products  11.7 us (1%)
    psum x1, waiting for transfers between devices, per_device(): gate_sum, up_sum = lax.psum((gate_part, up_part), 'grp')  284 us
    reduce_scatter x1, waiting for transfers between devices, per_device(): lax.psum_scatter(jnp.dot(attended, w_out, preferred_element_type=jnp.floa...  268 us
    all_to_all x1, waiting for transfers between devices, per_device(): lax.all_to_all(jnp.stack([prompt] * lax.axis_size('grp')), 'grp', 0, 0)  179 us
    all_gather x1, blocking collectives, per_device(): attended = lax.all_gather(own_rows, 'grp', axis=0, tiled=True)  155 us
    all_to_all x1, blocking collectives, per_device(): lax.all_to_all(outgoing, 'ctx', split_axis=0, concat_axis=1, tiled=True)  24.6 us
  transfers between devices with their start and end apart: 4, of which 4 were waited for; matrix products, arithmetic and copies ran while one was open for 0% of the time, Pallas kernels for 0%

profile of v1, /device:TPU:8, one launch (start us, length us, event | category | flops | bytes accessed | tf_op | source)
XLA Modules:
  0.0 1008.5 jit_solution(18087458745415093508)
XLA Ops:
  6.5 0.0 copy-start
  6.5 4.9 stack.2
  11.5 0.0 copy-start.4
  11.5 0.0 copy-start.7
  11.5 17.8 %all-to-all-start = ((bf16[16,384,576]{1,2,0:T(8,128)(2,1)}), bf16[16,384,576]{1,2,0:T(8,128)(2,1)}, u32[]{:S(2)}, u32[]{:S(2)}) async-start(bf16[16,384,576]{1,2,0:T(8,128)(2,1)} %stack.2), calls=%async_computation | async-start | bytes 14155776 | tf_op jit(solution)/shard_map/all_to_all | solution.py:36
  29.3 0.0 reduce-scatter.2.cloned.1.call-start
  29.4 0.0 copy-done.4
  29.4 0.0 copy-done.7
  29.4 0.5 fusion.3
  29.9 178.9 %all-to-all-done = bf16[16,384,576]{1,2,0:T(8,128)(2,1)} async-done(((bf16[16,384,576]{1,2,0:T(8,128)(2,1)}), bf16[16,384,576]{1,2,0:T(8,128)(2,1)}, u32[]{:S(2)}, u32[]{:S(2)}) %all-to-all-start) | async-done | bytes 7077920 | tf_op jit(solution)/shard_map/all_to_all | solution.py:36
  208.8 10.0 copy.22
  218.8 10.9 %reshape.82 = bf16[6144,576,1]{0,1,2:T(8,128)(2,1)} reshape(bf16[16,384,576]{1,0,2:T(8,128)(2,1)} %copy.22) | data formatting | bytes 14155776 | tf_op jit(solution)/shard_map/reshape | solution.py:35
  229.8 0.0 copy-start.1
  229.8 0.0 copy-start.8
  229.8 7.3 copy.34
  237.0 0.0 copy-done.1
  237.0 0.0 copy-done.8
  237.0 1.6 fusion.37
  238.7 0.4 fusion.1
  239.1 1.0 copy-done.2
  240.0 0.0 copy-start.6
  240.0 2.0 fusion
  242.1 0.0 copy-done.5
  242.1 0.0 copy-start.12
  242.1 0.0 copy-start.10
  242.1 0.3 fusion.7
  242.5 154.7 %all_gather.3 = bf16[256,512]{1,0:T(8,128)(2,1)S(1)} all-gather(bf16[16,512]{1,0:T(8,128)(2,1)S(1)} %bitcast.62), channel_id=1, replica_groups=mesh['ctx'=32,'grp'=16] {'grp'}, dimensions={0}, use_global_device_ids=true | all-gather | bytes 278528 | tf_op jit(solution)/shard_map/all_gather | solution.py:56
  397.2 0.0 copy-done.6
  397.2 1.1 fusion.38
  398.3 0.0 copy-start.3
  398.3 0.0 reduce-scatter.2.cloned.1.call-update
  398.3 0.0 all-reduce.3.cloned.1.call-start
  398.4 0.0 copy-done.12
  398.4 0.1 reshape.74
  398.4 0.1 fusion.24
  398.5 0.1 reduce_window_sum.11
  398.6 0.2 select_reduce_fusion
  398.8 0.3 convolution_convert_fusion.3
  399.1 268.4 %reduce-scatter.2.cloned.1.call-done = f32[8,448]{1,0:T(8,128)} async-done(((f32[256,448]{1,0:T(8,128)}), f32[8,448]{1,0:T(8,128)}) %reduce-scatter.2.cloned.1.call-update) | async-done | bytes 14352 | tf_op jit(solution)/shard_map/reduce_scatter | solution.py:58
  667.4 0.0 copy-done.10
  667.4 1.0 convolution_convert_fusion.2
  668.4 0.1 copy.26
  668.6 24.6 %all_to_all.23 = bf16[32,1,4,448]{3,2,1,0:T(4,128)(2,1)S(1)} all-to-all(bf16[32,1,4,448]{3,2,1,0:T(4,128)(2,1)S(1)} %bitcast.61), channel_id=1, replica_groups=mesh['ctx'=32,'grp'=16] {'ctx'}, dimensions={0} | all-to-all | bytes 229376 | tf_op jit(solution)/shard_map/all_to_all | solution.py:91
  693.2 0.0 copy-done
  693.2 1.1 convolution_bitcast_fusion
  694.3 0.0 copy-done.3
  694.3 0.0 copy-start.11
  694.3 0.0 copy-start.13
  694.3 1.1 convolution_bitcast_fusion.1
  695.4 0.0 all-reduce.3.cloned.1.call-update
  695.4 0.0 copy-done.11
  695.4 0.1 reduce_sum.29
  695.5 283.8 %all-reduce.3.cloned.1.call-done = (f32[1,32,4,1024]{3,1,2,0:T(8,128)}, f32[1,32,4,1024]{3,1,2,0:T(8,128)}) async-done(((f32[1,32,4,1024]{3,1,2,0:T(8,128)}, f32[1,32,4,1024]{3,1,2,0:T(8,128)}), (f32[1,32,4,1024]{3,1,2,0:T(8,128)}, f32[1,32,4,1024]{3,1,2,0:T(8,128)})) %all-reduce.3.cloned.1.call-update) | async-done | bytes 1048592 | tf_op jit(solution)/shard_map/psum | solution.py:96
  979.3 0.0 copy-done.13
  979.3 1.7 fusion.4
  981.0 0.8 copy.29
  981.7 7.0 all-to-all-start.2
  988.8 0.1 multiply_divide_fusion
  988.9 0.1 mul.53
  988.9 0.3 fusion.22
  989.2 11.6 %all-to-all-done.2 = bf16[1,32,4,448]{3,2,0,1:T(4,128)(2,1)S(1)} async-done(((bf16[1,32,4,448]{3,2,0,1:T(4,128)(2,1)}), bf16[1,32,4,448]{3,2,0,1:T(4,128)(2,1)S(1)}, u32[]{:S(2)}, u32[]{:S(2)}) %all-to-all-start.2) | async-done | bytes 114720 | tf_op jit(solution)/shard_map/all_to_all | solution.py:101
  1000.8 0.1 reshape.81
  1000.9 0.0 copy-done.9
  1000.9 0.8 fusion.8
  (6 shorter events, 0.1 us)
Async XLA Ops:
  6.5 686.6 %copy-start = (bf16[1,448,1024]{2,1,0:T(8,128)(2,1)S(1)}, bf16[1,448,1024]{2,1,0:T(8,128)(2,1)}, u32[]{:S(2)}) copy-start(bf16[1,448,1024]{2,1,0:T(8,128)(2,1)} %param.22) | copy-start | bytes 2752516
  11.5 17.9 %copy-start.4 = (bf16[4,128,512]{2,1,0:T(8,128)(2,1)S(1)}, bf16[4,128,512]{2,1,0:T(8,128)(2,1)}, u32[]{:S(2)}) copy-start(bf16[4,128,512]{2,1,0:T(8,128)(2,1)} %param.14) | copy-start | bytes 1572868
  11.5 17.9 %copy-start.7 = (bf16[256,4,128]{2,1,0:T(4,128)(2,1)S(1)}, bf16[256,4,128]{2,1,0:T(4,128)(2,1)}, u32[]{:S(2)}) copy-start(bf16[256,4,128]{2,1,0:T(4,128)(2,1)} %param.12) | copy-start | bytes 786436
  11.5 197.4 %all-to-all-start = ((bf16[16,384,576]{1,2,0:T(8,128)(2,1)}), bf16[16,384,576]{1,2,0:T(8,128)(2,1)}, u32[]{:S(2)}, u32[]{:S(2)}) async-start(bf16[16,384,576]{1,2,0:T(8,128)(2,1)} %stack.2), calls=%async_computation | async-start | bytes 14155776 | tf_op jit(solution)/shard_map/all_to_all | solution.py:36
  29.3 638.1 %reduce-scatter.2.cloned.1.call-start = ((), (), s32[]{:S(2)}) async-start(), calls=%async_computation.4 | async-start | bytes 540672 | tf_op jit(solution)/shard_map/reduce_scatter | solution.py:58
  229.8 7.3 copy-start.1
  229.8 7.3 copy-start.8
  237.0 3.0 copy-start.2
  240.0 2.0 copy-start.5
  240.0 157.1 %copy-start.6 = (bf16[512,448]{0,1:T(8,128)(2,1)S(1)}, bf16[512,448]{0,1:T(8,128)(2,1)}, u32[]{:S(2)}) copy-start(bf16[512,448]{0,1:T(8,128)(2,1)} %param.17) | copy-start | bytes 1376260
  242.1 156.3 %copy-start.12 = (s32[8,8]{1,0:T(8,128)S(1)}, s32[8,8]{1,0:T(8,128)}, u32[]{:S(2)}) copy-start(s32[8,8]{1,0:T(8,128)} %param.19) | copy-start | bytes 772
  242.1 425.3 %copy-start.10 = (bf16[8,448]{1,0:T(8,128)(2,1)S(1)}, bf16[8,448]{1,0:T(8,128)(2,1)}, u32[]{:S(2)}) copy-start(bf16[8,448]{1,0:T(8,128)(2,1)} %param.18) | copy-start | bytes 21508
  398.3 296.0 %copy-start.3 = (bf16[1,448,1024]{2,1,0:T(8,128)(2,1)S(1)}, bf16[1,448,1024]{2,1,0:T(8,128)(2,1)}, u32[]{:S(2)}) copy-start(bf16[1,448,1024]{2,1,0:T(8,128)(2,1)} %param.21) | copy-start | bytes 2752516
  398.3 581.0 %all-reduce.3.cloned.1.call-start = ((), (), s32[]{:S(2)}) async-start(), calls=%async_computation.5 | async-start | bytes 2097152 | tf_op jit(solution)/shard_map/psum | solution.py:96
  694.3 1.1 copy-start.11
  694.3 285.0 %copy-start.13 = (bf16[1,1024,448]{1,2,0:T(8,128)(2,1)S(1)}, bf16[1,1024,448]{1,2,0:T(8,128)(2,1)}, u32[]{:S(2)}) copy-start(bf16[1,1024,448]{1,2,0:T(8,128)(2,1)} %param.23) | copy-start | bytes 2752516
  979.3 21.5 %copy-start.9 = (f32[8,448]{1,0:T(8,128)S(1)}, f32[8,448]{1,0:T(8,128)}, u32[]{:S(2)}) copy-start(f32[8,448]{1,0:T(8,128)} %reduce-scatter.2.cloned.1.call-done) | copy-start | bytes 43012
  981.7 19.1 %all-to-all-start.2 = ((bf16[1,32,4,448]{3,2,0,1:T(4,128)(2,1)}), bf16[1,32,4,448]{3,2,0,1:T(4,128)(2,1)S(1)}, u32[]{:S(2)}, u32[]{:S(2)}) async-start(bf16[1,32,4,448]{3,2,0,1:T(4,128)(2,1)} %copy.29), calls=%async_computation.3 | async-start | bytes 262144 | tf_op jit(solution)/shard_map/all_to_all | solution.py:101
Sparse Core Ops, SparseCore 0:
  398.4 268.9 reduce-scatter.1
  695.5 283.7 all-reduce.2
